TPU v7x, 256 devices: a whole 4x4x8 slice. The times are simulated.
256 devices in a mesh: fsdp: 16 (over z, core), tensor: 16 (over y, x).
Axes of the slice: x: 4, y: 4, z: 8, core: 2. Of those that a mesh axis runs over, the one named last changes fastest.
Arguments:
- momentum: float32 [8192, 14336], P('fsdp', 'tensor'), may hold values from -1000 to 1000
- gradient: bfloat16 [8192, 14336], P('fsdp', 'tensor'), may hold values from -6 to 6
- right_state: float32 [14336, 256], P('tensor'), may hold values from -6 to 6
Outputs:
- momentum_next: float32 [8192, 14336], P('fsdp', 'tensor')
- right_next: float32 [14336, 256], P('tensor')
- step_direction: float32 [8192, 14336], P('fsdp', 'tensor')
All inputs are finite; a program needn't handle non-finite values.
Results may differ from a plain program's by a relative error of at most 0.0003.
Values sent between devices are 32-bit elements; how exact they have to be, the bound alone decides.
No kernel may reach another device: no remote copies, remote signals or barrier semaphores. Data moves between devices by JAX's collectives and lax.ppermute only.
A program may use at most 64 MiB of HBM per device.

v0:
```python
import math

import jax
import jax.numpy as jnp
from jax import lax
from jax.experimental import pallas as pl
from jax.experimental.pallas import tpu as pltpu
from jax.sharding import PartitionSpec as P

D = 8192
FFW = 14336
RANK = 256
BLOCK = 64
VMEM = 20 * 2**20
TENSOR = 16
Z = 8

highest = lax.Precision.HIGHEST
error_share = 0.05
z_groups = [[2 * z + core for z in range(Z)] for core in range(2)]


def multiply(left_side, right_side, left_dim, right_dim, precision=highest):
    return lax.dot_general(
        left_side,
        right_side,
        (((left_dim,), (right_dim,)), ((), ())),
        precision=precision,
        preferred_element_type=jnp.float32,
    )


def spread_lane(tile, lane):
    return jnp.take_along_axis(tile, jnp.full(tile.shape, lane, jnp.int32), axis=1)


def spread_row(tile, row):
    return jnp.broadcast_to(tile[row : row + 1, :], tile.shape)


def factor_block(tiles, first_lane, row_index):
    tiles = list(tiles)
    count = len(tiles)
    own = [spread_lane(tiles[0], first_lane + j) for j in range(8)]
    for s in range(count):
        below = range(s + 1, count)
        columns = [
            {i: spread_lane(tiles[i], first_lane + 8 * s + j) for i in below} for j in range(8)
        ]
        if below:
            following = [
                spread_lane(tiles[s + 1], first_lane + 8 * (s + 1) + j) for j in range(8)
            ]
        steps, own_steps, pivots = [], [], None
        for k in range(8):
            pivot = spread_row(own[k], k)
            inverse_pivot = 1.0 / pivot
            pivots = pivot if pivots is None else jnp.where(row_index == k, pivot, pivots)
            own_step = own[k] * inverse_pivot
            step = {i: columns[k][i] * inverse_pivot for i in below}
            own_steps.append(jnp.where(row_index > k, own_step, 0.0))
            steps.append(step)
            for j in range(k + 1, 8):
                entry = spread_row(own[j], k)
                own[j] = own[j] - own_step * entry
                for i in below:
                    columns[j][i] = columns[j][i] - step[i] * entry
            if below:
                for j in range(8):
                    following[j] = following[j] - step[s + 1] * spread_row(columns[k][s + 1], j)
        tile = tiles[s]
        for k in range(8):
            pivot_row = spread_row(tile, k)
            tile = tile - own_steps[k] * pivot_row
            for i in below:
                tiles[i] = tiles[i] - steps[k][i] * pivot_row
        tiles[s] = tile * lax.rsqrt(pivots)
        own = following
    return tiles


def deep_multiply(left_side, right_side):
    high, middle, low = terms(left_side, 3)
    left = jnp.concatenate([low, high, middle, middle, high, high], axis=1)
    high, middle, low = terms(right_side, 3)
    right = jnp.concatenate([high, low, middle, high, middle, high], axis=0)
    return multiply(left, right, 1, 0, None)


def invert_factor(gram, work_ref, inverse_ref):
    rows = lax.broadcasted_iota(jnp.int32, (RANK, RANK), 0)
    lanes = lax.broadcasted_iota(jnp.int32, (RANK, RANK), 1)
    diagonal = rows == lanes
    ridge = (1e-06 / RANK) * jnp.sum(jnp.where(diagonal, gram, 0.0), keepdims=True)
    work_ref[:, :RANK] = gram + jnp.where(diagonal, ridge, 0.0)
    work_ref[:, RANK:] = jnp.where(diagonal, 1.0, 0.0)
    row_index = lax.broadcasted_iota(jnp.int32, (8, 128), 0)
    lane_index = lax.broadcasted_iota(jnp.int32, (8, 128), 1)
    for block in range(RANK // BLOCK):
        top = block * BLOCK
        aligned = top // 128 * 128
        first_lane = top - aligned
        own_half = lane_index >= 64 if first_lane else lane_index < 64
        tiles = []
        for i in range(BLOCK // 8):
            part = work_ref[top + 8 * i : top + 8 * i + 8, aligned : aligned + 128]
            unit = jnp.where(lane_index == row_index + (8 * i + 64 - first_lane), 1.0, 0.0)
            tiles.append(jnp.where(own_half, part, unit))
        factored = jnp.concatenate(factor_block(tiles, first_lane, row_index), axis=0)
        if first_lane == 0:
            factored = pltpu.roll(factored, 64, 1)
        below = top + BLOCK
        start = RANK if below == RANK else below // 128 * 128
        width = -(-below // 128) * 128
        stop = RANK + width
        done = deep_multiply(factored[:, :BLOCK], work_ref[top:below, start:stop])
        inverse_ref[top:below, :width] = done[:, RANK - start :]
        if width < RANK:
            inverse_ref[top:below, width:] = jnp.zeros((BLOCK, RANK - width), jnp.float32)
        if below < RANK:
            update = deep_multiply(done[:, : RANK - start].T, done)
            work_ref[below:, start:stop] = work_ref[below:, start:stop] - update[below - start :, :]


def terms(value, count):
    found = []
    for left in range(count - 1, -1, -1):
        term = value.astype(jnp.bfloat16)
        found.append(term)
        if left:
            value = value - term.astype(jnp.float32)
    return found


CHUNKS = 4


def term_multiply(left_terms, right_terms, right_dim=0):
    count = len(right_terms)
    rows = left_terms[0].shape[0]
    total = None
    for order in range(count - 1, -1, -1):
        met = left_terms[: count - order]
        stack = met[0] if len(met) == 1 else jnp.concatenate(met, axis=0)
        product = multiply(stack, right_terms[order], 1, right_dim, None)
        for i in range(len(met) - 1, -1, -1):
            part = product[i * rows : (i + 1) * rows]
            total = part if total is None else total + part
    return total


def pack_gram(rows, quarter, row_lane):
    turned = rows
    for i in range(1, 4):
        turned = jnp.where(quarter == i, pltpu.roll(rows, RANK - 64 * i, 1), turned)
    tiles = [turned[8 * i : 8 * i + 8, :128] for i in range(4)]
    for i in (0, 2):
        first, second = (turned[8 * k : 8 * k + 8, 128:] for k in (i, i + 1))
        tiles.append(jnp.where(row_lane < 64, first, pltpu.roll(second, 64, 1)))
    return tiles


def unpack_gram(tiles, row_lane):
    rows = []
    for i in range(4):
        near = tiles[i] * jnp.where(row_lane < 64, 0.5, 1.0)
        far = tiles[4 + i // 2]
        far = pltpu.roll(far, 64, 1) if i % 2 else far
        rows.append(jnp.concatenate([near, jnp.where(row_lane < 64, 0.5 * far, 0.0)], axis=1))
    return rows


def own_place():
    return lax.rem(lax.axis_index("tensor"), 4), lax.rem(lax.axis_index("fsdp"), 2)


def left_kernel(
    momentum_ref, gradient_ref, state_ref, out_ref,
    held_momentum, held_gradient, held_state, arrived,
):
    width = held_momentum.shape[1]
    chunks = []
    for i, start in enumerate(range(0, width, RANK)):
        part = pl.ds(start, min(RANK, width - start))
        fetches = (
            pltpu.make_async_copy(state_ref.at[part], held_state.at[part], arrived.at[3 * i]),
            pltpu.make_async_copy(
                momentum_ref.at[:, part], held_momentum.at[:, part], arrived.at[3 * i + 1]
            ),
            pltpu.make_async_copy(
                gradient_ref.at[:, part], held_gradient.at[:, part], arrived.at[3 * i + 2]
            ),
        )
        for fetch in fetches:
            fetch.start()
        chunks.append((part, fetches))
    total = None
    for part, fetches in chunks:
        for fetch in fetches:
            fetch.wait()
        buffer = held_momentum[:, part] + held_gradient[:, part].astype(jnp.float32)
        product = term_multiply(terms(buffer, 3), terms(held_state[part, :], 3))
        total = product if total is None else total + product
    out_ref[...] = total


def first_kernel(
    gram_ref, left_ref, momentum_ref, gradient_ref,
    once_ref, kept_ref, given_ref, work_ref, inverse_ref, square_ref, right_ref,
    held_momentum, held_gradient, arrived,
):
    quarter, core = own_place()
    fetches = (
        pltpu.make_async_copy(momentum_ref, held_momentum, arrived.at[0]),
        pltpu.make_async_copy(gradient_ref, held_gradient, arrived.at[1]),
    )
    for fetch in fetches:
        fetch.start()
    invert_factor(gram_ref[...], work_ref, inverse_ref)
    once = multiply(left_ref[...], inverse_ref[...], 1, 1)
    once_ref[...] = once
    turned = terms(once.T, 3)
    square_ref[...] = term_multiply(turned, turned, 1)
    for fetch in fetches:
        fetch.wait()
    buffer = held_momentum[...] + held_gradient[...].astype(jnp.float32)
    right_ref[...] = term_multiply(turned, terms(buffer, 3)).T
    row_lane = lax.broadcasted_iota(jnp.int32, (8, 128), 1)
    size = right_ref.shape[0] // 2
    for target, half in ((kept_ref, core), (given_ref, 1 - core)):
        target[:size, :] = right_ref[pl.ds(pl.multiple_of(half * size, 8), size), :]
        start = pl.multiple_of(quarter * 64 + half * 32, 32)
        tiles = pack_gram(square_ref[pl.ds(start, 32), :], quarter, row_lane)
        for i, tile in enumerate(tiles):
            top, left = size + i // 2 * 8, i % 2 * 128
            target[top : top + 8, left : left + 128] = tile


def second_kernel(own_ref, other_ref, once_ref, found_ref, gram_ref, work_ref):
    rows = once_ref.shape[0]
    inverse_ref = found_ref.at[rows:]
    quarter, core = own_place()
    row_lane = lax.broadcasted_iota(jnp.int32, (8, 128), 1)
    for step in range(4):
        base = lax.rem(quarter + (4 - step), 4) * 64
        for source, half in ((own_ref, core), (other_ref, 1 - core)):
            tiles = [
                source[24 * step + top : 24 * step + top + 8, left : left + 128]
                for top in (0, 8, 16)
                for left in (0, 128)
            ]
            start = pl.multiple_of(base + half * 32, 32)
            for i, part in enumerate(unpack_gram(tiles, row_lane)):
                gram_ref[pl.ds(start + 8 * i, 8), :] = part
    parts = [gram_ref[64 * i : 64 * i + 64, :] for i in range(4)]
    parts = [parts[0]] + [pltpu.roll(parts[i], 64 * i, 1) for i in range(1, 4)]
    gram = jnp.concatenate(parts, axis=0)
    invert_factor(gram + gram.T, work_ref, inverse_ref)
    found_ref[:rows, :] = multiply(once_ref[...], inverse_ref[...], 1, 1)


def third_kernel(part_ref, found_ref, right_ref, square_ref):
    inverse = found_ref[found_ref.shape[0] - RANK :, :]
    right = multiply(part_ref[...], inverse, 1, 1)
    right_ref[...] = right
    squares = jnp.sum(right * right, axis=0, keepdims=True)
    for i in range(square_ref.shape[0]):
        square_ref[i] = squares


def lay_together(core, own_ref, other_ref, whole_ref):
    size = own_ref.shape[0]
    for source, half in ((own_ref, core), (other_ref, 1 - core)):
        whole_ref[pl.ds(pl.multiple_of(half * size, 8), size), :] = source[...]


def fourth_kernel(
    momentum_ref, gradient_ref, found_ref, own_ref, other_ref,
    next_ref, held_momentum, held_gradient, right_ref, arrived,
):
    fetches = (
        pltpu.make_async_copy(momentum_ref, held_momentum, arrived.at[0]),
        pltpu.make_async_copy(gradient_ref, held_gradient, arrived.at[1]),
    )
    for fetch in fetches:
        fetch.start()
    lay_together(own_place()[1], own_ref, other_ref, right_ref)
    basis = found_ref[: next_ref.shape[0], :]
    product = term_multiply(terms(basis, 2), terms(right_ref[...], 2), 1)
    for fetch in fetches:
        fetch.wait()
    buffer = held_momentum[...] + held_gradient[...].astype(jnp.float32)
    next_ref[...] = buffer - error_share * product


def fifth_kernel(
    squares_ref, found_ref, own_ref, other_ref, next_ref, step_ref,
    next_held, step_held, right_ref, done,
):
    lay_together(own_place()[1], own_ref, other_ref, right_ref)
    square_sum = squares_ref[0]
    for i in range(1, squares_ref.shape[0]):
        square_sum = square_sum + squares_ref[i]
    scale = lax.rsqrt(square_sum * (1.0 / FFW) + 1e-06)
    next_held[...] = right_ref[...] * scale
    writes = [pltpu.make_async_copy(next_held, next_ref, done.at[CHUNKS])]
    writes[0].start()
    rows, width = step_held.shape
    left = terms(found_ref[:rows, :] * (scale * math.sqrt(D / RANK)), 2)
    for i, start in enumerate(range(0, width, RANK)):
        columns = pl.ds(start, min(RANK, width - start))
        step_held[:, columns] = term_multiply(left, terms(right_ref[columns, :].T, 2))
        writes.append(
            pltpu.make_async_copy(step_held.at[:, columns], step_ref.at[:, columns], done.at[i])
        )
        writes[-1].start()
    for write in writes:
        write.wait()


def sum_kernel(parts_ref, copies_ref, rest_ref=None):
    total = parts_ref[0]
    for i in range(1, parts_ref.shape[0]):
        total = total + parts_ref[i]
    height = copies_ref.shape[1]
    for i in range(copies_ref.shape[0]):
        copies_ref[i] = total[:height]
    if rest_ref is not None:
        rest_ref[...] = total[height:]


def call(kernel, name, operands, outputs, scratch=(), far=(), near=(), out_far=()):
    operands = list(operands)
    in_specs = [pl.BlockSpec(memory_space=pltpu.VMEM)] * len(operands)
    for i in far:
        operands[i] = pltpu.with_memory_space_constraint(operands[i], pltpu.HBM)
        in_specs[i] = pl.BlockSpec(memory_space=pl.ANY)
    out_shape, out_specs = [], []
    for i, output in enumerate(outputs):
        shape, dtype = output if isinstance(output[0], tuple) else (output, jnp.float32)
        out_shape.append(
            pltpu.VMEM(shape, dtype) if i in near else jax.ShapeDtypeStruct(shape, dtype)
        )
        space = pl.ANY if i in out_far else pltpu.VMEM
        out_specs.append(pl.BlockSpec(memory_space=space))
    return pl.pallas_call(
        kernel,
        out_shape=out_shape,
        in_specs=in_specs,
        out_specs=out_specs,
        scratch_shapes=list(scratch),
        compiler_params=pltpu.CompilerParams(vmem_limit_bytes=VMEM),
        cost_estimate=pl.CostEstimate(
            flops=10**9, bytes_accessed=8 * 2**20, transcendentals=0
        ),
        name=name,
    )(*operands)


def room(*shape, dtype=jnp.float32):
    return pltpu.VMEM(shape, dtype)


plane_groups = [
    [(2 * z + core) * TENSOR + t for t in range(TENSOR) for core in range(2)] for z in range(Z)
]
both_axes = ("fsdp", "tensor")


def exchange(block, axis, groups=None):
    return lax.all_to_all(block, axis, 0, 0, axis_index_groups=groups, tiled=True)


def copies(block, members):
    return jnp.broadcast_to(block, (members,) + block.shape)


def swap_cores(block):
    return lax.ppermute(block, "fsdp", [(i, i ^ 1) for i in range(2 * Z)])


def core_half(block, core):
    half = block.shape[0] // 2
    kept = lax.dynamic_slice_in_dim(block, core * half, half)
    given = lax.dynamic_slice_in_dim(block, (1 - core) * half, half)
    return kept + swap_cores(given)


def gram_rows(factor, place):
    width = RANK // TENSOR
    own = lax.dynamic_slice_in_dim(factor, place * width, width, axis=1)
    return multiply(own, factor, 0, 0)


def per_device(momentum, gradient, right_state):
    core = lax.axis_index("fsdp") % 2
    place = lax.axis_index("tensor")
    rows, columns = momentum.shape
    held = [room(rows, columns), room(rows, columns, dtype=gradient.dtype)]
    (partial_left,) = call(
        left_kernel,
        "left",
        (momentum, gradient, right_state),
        ((rows, RANK),),
        held + [room(columns, RANK), pltpu.SemaphoreType.DMA((3 * CHUNKS,))],
        far=(0, 1, 2),
    )
    parts = exchange(partial_left.reshape(TENSOR, rows // TENSOR, RANK), "tensor")
    (parts,) = call(sum_kernel, "left_sum", (parts,), (parts.shape,))
    left_raw = exchange(parts, "tensor").reshape(rows, RANK)

    gram_part = core_half(gram_rows(left_raw, place), core)
    parts = exchange(copies(gram_part, Z), "fsdp", z_groups)
    (parts,) = call(
        sum_kernel, "gram_sum", (parts,), ((2 * TENSOR,) + parts.shape[1:],)
    )
    gram = exchange(parts, both_axes, plane_groups).reshape(RANK, RANK)
    work = [room(RANK, 2 * RANK), room(RANK, RANK)]
    left_once, kept, given = call(
        first_kernel,
        "first",
        (gram, left_raw, momentum, gradient),
        ((rows, RANK), (columns // 2 + 24, RANK), (columns // 2 + 24, RANK)),
        work + [room(RANK, RANK), room(columns, RANK)] + held + [pltpu.SemaphoreType.DMA((2,))],
        far=(2, 3),
        near=(0,),
    )

    part = kept + swap_cores(given)
    size = columns // 2
    parts = jnp.concatenate(
        [part[:size].reshape(Z, size // Z, RANK), copies(part[size:], Z)], axis=1
    )
    parts = exchange(parts, "fsdp", z_groups)
    parts, gram_part = call(
        sum_kernel, "right_sum", (parts,), ((Z, size // Z, RANK), (24, RANK))
    )
    right_part = exchange(parts, "fsdp", z_groups)
    received = [gram_part]
    for step in range(1, 4):
        pairs = [(i, i // 4 * 4 + (i + step) % 4) for i in range(TENSOR)]
        received.append(lax.ppermute(gram_part, "tensor", pairs))
    gram_part = jnp.concatenate(received, axis=0)
    (found,) = call(
        second_kernel,
        "second",
        (gram_part, swap_cores(gram_part), left_once),
        ((rows + RANK, RANK),),
        (work[1], work[0]),
        near=(0,),
    )
    right_part, found = lax.optimization_barrier((right_part, found))
    right_part, squares = call(
        third_kernel,
        "third",
        (right_part.reshape(size, RANK), found),
        ((size, RANK), (2 * TENSOR, 1, RANK)),
        near=(0,),
    )
    squares = exchange(squares, both_axes, plane_groups)
    other_part = swap_cores(right_part)
    (momentum_next,) = call(
        fourth_kernel,
        "fourth",
        (momentum, gradient, found, right_part, other_part),
        ((rows, columns),),
        held + [room(columns, RANK), pltpu.SemaphoreType.DMA((2,))],
        far=(0, 1),
    )
    right_next, step_direction = call(
        fifth_kernel,
        "fifth",
        (squares, found, right_part, other_part),
        ((columns, RANK), (rows, columns)),
        [room(columns, RANK), room(rows, columns), room(columns, RANK), pltpu.SemaphoreType.DMA((CHUNKS + 1,))],
        out_far=(0, 1),
    )
    return (momentum_next, right_next, step_direction)


def solution(mesh):
    return jax.shard_map(
        per_device,
        mesh=mesh,
        in_specs=(P("fsdp", "tensor"), P("fsdp", "tensor"), P("tensor", None)),
        out_specs=(P("fsdp", "tensor"), P("tensor", None), P("fsdp", "tensor")),
        check_vma=False,
    )
```

profile of v0, /device:TPU:1, one launch (start us, length us, event | category | flops | bytes accessed | tf_op | source)
XLA Modules:
  0.0 140.9 jit_solution(599004395529269724)
XLA Ops:
  0.6 3.6 %left.1 = f32[512,256]{1,0:T(8,128)S(1)} custom-call(f32[512,896]{1,0:T(8,128)} %momentum_ref.5, bf16[512,896]{1,0:T(8,128)(2,1)} %gradient_ref.5, f32[896,256]{1,0:T(8,128)} %state_ref.1), custom_call_target="tpu_custom_call" | custom-call | flops 1000000000 | bytes 8388608 | tf_op jit(solution)/shard_map/left/pallas_call | solution.py:346
  4.2 17.9 %all_to_all.35.parts_ref = f32[16,32,256]{2,1,0:T(8,128)S(1)} all-to-all(f32[16,32,256]{2,1,0:T(8,128)S(1)} %bitcast.8), channel_id=1, replica_groups=mesh['fsdp'=16,'tensor'=16] {'tensor'}, dimensions={0} | all-to-all | bytes 1048576 | tf_op jit(solution)/shard_map/all_to_all | solution.py:371
  22.1 0.9 left_sum.1
  23.0 3.6 %all-to-all-start.1 = ((f32[16,32,256]{2,1,0:T(8,128)}), f32[16,32,256]{2,1,0:T(8,128)S(1)}, u32[]{:S(2)}, u32[]{:S(2)}) async-start(f32[16,32,256]{2,1,0:T(8,128)} %left_sum.1), calls=%async_computation.1 | async-start | bytes 1048576 | tf_op jit(solution)/shard_map/all_to_all | solution.py:371
  26.6 9.6 %all-to-all-done.1 = f32[16,32,256]{2,1,0:T(8,128)S(1)} async-done(((f32[16,32,256]{2,1,0:T(8,128)}), f32[16,32,256]{2,1,0:T(8,128)S(1)}, u32[]{:S(2)}, u32[]{:S(2)}) %all-to-all-start.1) | async-done | bytes 524320 | tf_op jit(solution)/shard_map/all_to_all | solution.py:371
  36.2 0.6 fusion
  36.9 2.9 %collective-permute-start = (f32[8,256]{1,0:T(8,128)S(1)}, f32[8,256]{1,0:T(8,128)S(1)}, u32[]{:S(2)}, u32[]{:S(2)}) collective-permute-start(f32[8,256]{1,0:T(8,128)S(1)} %constant_dynamic-slice_fusion), channel_id=1, source_target_pairs={{0,16},{16,0},{32,48},{48,32},{64,80},{80,64},{96,112},{112,96},{1... | collective-permute-start | bytes 24584 | tf_op jit(solution)/shard_map/ppermute | solution.py:379
  39.8 0.8 collective-permute-done
  40.7 15.2 %all_to_all.36.parts_ref = f32[8,8,256]{2,1,0:T(8,128)S(1)} all-to-all(f32[8,8,256]{2,1,0:T(8,128)S(1)} %broadcast_in_dim.6), channel_id=1, replica_groups={{0,32,64,96,128,160,192,224},{16,48,80,112,144,176,208,240},{1,33,65,97..., dimensions={0} | all-to-all | bytes 131072 | tf_op jit(solution)/shard_map/all_to_all | solution.py:371
  55.9 13.6 %all_to_all.37 = f32[32,8,256]{2,1,0:T(8,128)S(1)} all-to-all(f32[32,8,256]{2,1,0:T(8,128)S(1)} %gram_sum.1), channel_id=1, replica_groups={{0,16,1,17,2,18,3,19,4,20,5,21,6,22,7,23,8,24,9,25,10,26,11,27,12,28,13..., dimensions={0} | all-to-all | bytes 524288 | tf_op jit(solution)/shard_map/all_to_all | solution.py:371
  69.5 10.1 %first.1 = (f32[512,256]{1,0:T(8,128)S(1)}, f32[472,256]{1,0:T(8,128)S(1)}, f32[472,256]{1,0:T(8,128)S(1)}) custom-call(f32[256,256]{1,0:T(8,128)S(1)} %bitcast.10, f32[512,256]{1,0:T(8,128)S(1)} %bitcast.7, f32[512,896]{1,0:T(8,128)} %momentum_ref.5, bf16[512,896]{1,0:T(8,128)(2,1)} %gradient_ref.5), custom_call_target="tpu_custom_call" | custom-call | flops 1000000000 | bytes 8388608 | tf_op jit(solution)/shard_map/first/pallas_call | solution.py:346
  79.6 0.5 collective-permute-start.1
  80.1 1.6 %collective-permute-done.1 = f32[472,256]{1,0:T(8,128)S(1)} collective-permute-done((f32[472,256]{1,0:T(8,128)S(1)}, f32[472,256]{1,0:T(8,128)S(1)}, u32[]{:S(2)}, u32[]{:S(2)}) %collective-permute-start.1) | collective-permute-done | bytes 483360 | tf_op jit(solution)/shard_map/ppermute | solution.py:379
  81.7 0.1 add.24
  81.9 0.1 pad_maximum_fusion
  81.9 23.2 %all_to_all.38.parts_ref = f32[8,80,256]{2,1,0:T(8,128)S(1)} all-to-all(f32[8,80,256]{2,1,0:T(8,128)S(1)} %pad_maximum_fusion), channel_id=1, replica_groups={{0,32,64,96,128,160,192,224},{16,48,80,112,144,176,208,240},{1,33,65,97..., dimensions={0} | all-to-all | bytes 1310720 | tf_op jit(solution)/shard_map/all_to_all | solution.py:371
  105.1 0.8 right_sum.1
  105.9 3.5 %all-to-all-start.5 = ((f32[8,56,256]{2,1,0:T(8,128)}), f32[8,56,256]{2,1,0:T(8,128)S(1)}, u32[]{:S(2)}, u32[]{:S(2)}) async-start(f32[8,56,256]{2,1,0:T(8,128)} %get-tuple-element.16), calls=%async_computation.5 | async-start | bytes 917504 | tf_op jit(solution)/shard_map/all_to_all | solution.py:371
  109.4 0.6 collective-permute-start.2
  110.0 1.8 %collective-permute-start.3 = (f32[24,256]{1,0:T(8,128)S(1)}, f32[24,256]{1,0:T(8,128)S(1)}, u32[]{:S(2)}, u32[]{:S(2)}) collective-permute-start(f32[24,256]{1,0:T(8,128)S(1)} %get-tuple-element.17), channel_id=1, source_target_pairs={{0,2},{1,3},{2,0},{3,1},{4,6},{5,7},{6,4},{7,5},{8,10},{9,11},{10,... | collective-permute-start | bytes 73736 | tf_op jit(solution)/shard_map/ppermute | solution.py:442
  111.8 0.7 collective-permute-start.4
  112.5 0.9 collective-permute-done.2
  113.4 0.9 collective-permute-done.3
  114.2 0.6 collective-permute-done.4
  114.8 1.9 %collective-permute-start.5 = (f32[96,256]{1,0:T(8,128)S(1)}, f32[96,256]{1,0:T(8,128)S(1)}, u32[]{:S(2)}, u32[]{:S(2)}) collective-permute-start(f32[96,256]{1,0:T(8,128)S(1)} %constant_dynamic-update-slice_fusion.own_ref), channel_id=1, source_target_pairs={{0,16},{16,0},{32,48},{48,32},{64,80},{80,64},{96,112},{112,96},{1... | collective-permute-start | bytes 294920 | tf_op jit(solution)/shard_map/ppermute | solution.py:379
  116.7 0.9 collective-permute-done.5.other_ref
  117.6 6.9 %second.1.found_ref = f32[768,256]{1,0:T(8,128)S(1)} custom-call(f32[96,256]{1,0:T(8,128)S(1)} %constant_dynamic-update-slice_fusion.own_ref, f32[96,256]{1,0:T(8,128)S(1)} %collective-permute-done.5.other_ref, f32[512,256]{1,0:T(8,128)S(1)} %get-tuple-element.18.once_ref), custom_call_target="tpu_custom_call" | custom-call | flops 1000000000 | bytes 8388608 | tf_op jit(solution)/shard_map/second/pallas_call | solution.py:346
  124.5 1.3 all-to-all-done.5
  125.9 1.2 third.1
  127.1 0.5 collective-permute-start.6
  127.6 3.6 %all-to-all-start.6 = ((f32[32,1,256]{2,1,0:T(1,128)}), f32[32,1,256]{2,1,0:T(1,128)S(1)}, u32[]{:S(2)}, u32[]{:S(2)}) async-start(f32[32,1,256]{2,1,0:T(1,128)} %get-tuple-element.22), calls=%async_computation.6 | async-start | bytes 65536 | tf_op jit(solution)/shard_map/all_to_all | solution.py:371
  131.2 0.0 collective-permute-done.6.other_ref
  131.2 3.7 %fourth.1 = f32[512,896]{1,0:T(8,128)} custom-call(f32[512,896]{1,0:T(8,128)} %momentum_ref.5, bf16[512,896]{1,0:T(8,128)(2,1)} %gradient_ref.5, f32[768,256]{1,0:T(8,128)S(1)} %second.1.found_ref, f32[448,256]{1,0:T(8,128)S(1)} %get-tuple-element.21.own_ref, f32[448,256]{1,0:T(8,128)S(1)} %collective-permute-done.6.other_ref), custom_call_target="tpu_custom_call" | custom-call | flops 1000000000 | bytes 8388608 | tf_op jit(solution)/shard_map/fourth/pallas_call | solution.py:346
  134.9 3.5 %all-to-all-done.6.squares_ref = f32[32,1,256]{2,1,0:T(1,128)S(1)} async-done(((f32[32,1,256]{2,1,0:T(1,128)}), f32[32,1,256]{2,1,0:T(1,128)S(1)}, u32[]{:S(2)}, u32[]{:S(2)}) %all-to-all-start.6) | async-done | bytes 32800 | tf_op jit(solution)/shard_map/all_to_all | solution.py:371
  138.5 2.3 %fifth.1 = (f32[896,256]{1,0:T(8,128)}, f32[512,896]{1,0:T(8,128)}) custom-call(f32[32,1,256]{2,1,0:T(1,128)S(1)} %all-to-all-done.6.squares_ref, f32[768,256]{1,0:T(8,128)S(1)} %second.1.found_ref, f32[448,256]{1,0:T(8,128)S(1)} %get-tuple-element.21.own_ref, f32[448,256]{1,0:T(8,128)S(1)} %collective-permute-done.6.other_ref), custom_call_target="tpu_custom_call" | custom-call | flops 1000000000 | bytes 8388608 | tf_op jit(solution)/shard_map/fifth/pallas_call | solution.py:346
  (11 shorter events, 0.1 us)
Async XLA Ops:
  23.0 13.2 %all-to-all-start.1 = ((f32[16,32,256]{2,1,0:T(8,128)}), f32[16,32,256]{2,1,0:T(8,128)S(1)}, u32[]{:S(2)}, u32[]{:S(2)}) async-start(f32[16,32,256]{2,1,0:T(8,128)} %left_sum.1), calls=%async_computation.1 | async-start | bytes 1048576 | tf_op jit(solution)/shard_map/all_to_all | solution.py:371
  36.9 3.8 %collective-permute-start = (f32[8,256]{1,0:T(8,128)S(1)}, f32[8,256]{1,0:T(8,128)S(1)}, u32[]{:S(2)}, u32[]{:S(2)}) collective-permute-start(f32[8,256]{1,0:T(8,128)S(1)} %constant_dynamic-slice_fusion), channel_id=1, source_target_pairs={{0,16},{16,0},{32,48},{48,32},{64,80},{80,64},{96,112},{112,96},{1... | collective-permute-start | bytes 24584 | tf_op jit(solution)/shard_map/ppermute | solution.py:379
  79.6 2.1 %collective-permute-start.1 = (f32[472,256]{1,0:T(8,128)S(1)}, f32[472,256]{1,0:T(8,128)S(1)}, u32[]{:S(2)}, u32[]{:S(2)}) collective-permute-start(f32[472,256]{1,0:T(8,128)S(1)} %get-tuple-element.15), channel_id=1, source_target_pairs={{0,16},{16,0},{32,48},{48,32},{64,80},{80,64},{96,112},{112,96},{1... | collective-permute-start | bytes 1449992 | tf_op jit(solution)/shard_map/ppermute | solution.py:379
  105.9 20.0 %all-to-all-start.5 = ((f32[8,56,256]{2,1,0:T(8,128)}), f32[8,56,256]{2,1,0:T(8,128)S(1)}, u32[]{:S(2)}, u32[]{:S(2)}) async-start(f32[8,56,256]{2,1,0:T(8,128)} %get-tuple-element.16), calls=%async_computation.5 | async-start | bytes 917504 | tf_op jit(solution)/shard_map/all_to_all | solution.py:371
  109.4 4.0 %collective-permute-start.2 = (f32[24,256]{1,0:T(8,128)S(1)}, f32[24,256]{1,0:T(8,128)S(1)}, u32[]{:S(2)}, u32[]{:S(2)}) collective-permute-start(f32[24,256]{1,0:T(8,128)S(1)} %get-tuple-element.17), channel_id=1, source_target_pairs={{0,1},{1,2},{2,3},{3,0},{4,5},{5,6},{6,7},{7,4},{8,9},{9,10},{10,1... | collective-permute-start | bytes 73736 | tf_op jit(solution)/shard_map/ppermute | solution.py:442
  110.0 4.2 %collective-permute-start.3 = (f32[24,256]{1,0:T(8,128)S(1)}, f32[24,256]{1,0:T(8,128)S(1)}, u32[]{:S(2)}, u32[]{:S(2)}) collective-permute-start(f32[24,256]{1,0:T(8,128)S(1)} %get-tuple-element.17), channel_id=1, source_target_pairs={{0,2},{1,3},{2,0},{3,1},{4,6},{5,7},{6,4},{7,5},{8,10},{9,11},{10,... | collective-permute-start | bytes 73736 | tf_op jit(solution)/shard_map/ppermute | solution.py:442
  111.8 3.0 %collective-permute-start.4 = (f32[24,256]{1,0:T(8,128)S(1)}, f32[24,256]{1,0:T(8,128)S(1)}, u32[]{:S(2)}, u32[]{:S(2)}) collective-permute-start(f32[24,256]{1,0:T(8,128)S(1)} %get-tuple-element.17), channel_id=1, source_target_pairs={{0,3},{1,0},{2,1},{3,2},{4,7},{5,4},{6,5},{7,6},{8,11},{9,8},{10,9... | collective-permute-start | bytes 73736 | tf_op jit(solution)/shard_map/ppermute | solution.py:442
  114.8 2.8 %collective-permute-start.5 = (f32[96,256]{1,0:T(8,128)S(1)}, f32[96,256]{1,0:T(8,128)S(1)}, u32[]{:S(2)}, u32[]{:S(2)}) collective-permute-start(f32[96,256]{1,0:T(8,128)S(1)} %constant_dynamic-update-slice_fusion.own_ref), channel_id=1, source_target_pairs={{0,16},{16,0},{32,48},{48,32},{64,80},{80,64},{96,112},{112,96},{1... | collective-permute-start | bytes 294920 | tf_op jit(solution)/shard_map/ppermute | solution.py:379
  127.1 4.1 %collective-permute-start.6 = (f32[448,256]{1,0:T(8,128)S(1)}, f32[448,256]{1,0:T(8,128)S(1)}, u32[]{:S(2)}, u32[]{:S(2)}) collective-permute-start(f32[448,256]{1,0:T(8,128)S(1)} %get-tuple-element.21.own_ref), channel_id=1, source_target_pairs={{0,16},{16,0},{32,48},{48,32},{64,80},{80,64},{96,112},{112,96},{1... | collective-permute-start | bytes 1376264 | tf_op jit(solution)/shard_map/ppermute | solution.py:379
  127.6 10.9 %all-to-all-start.6 = ((f32[32,1,256]{2,1,0:T(1,128)}), f32[32,1,256]{2,1,0:T(1,128)S(1)}, u32[]{:S(2)}, u32[]{:S(2)}) async-start(f32[32,1,256]{2,1,0:T(1,128)} %get-tuple-element.22), calls=%async_computation.6 | async-start | bytes 65536 | tf_op jit(solution)/shard_map/all_to_all | solution.py:371
where the time goes:
time: 141 us
  blocking collectives  69.9 us (50%)
  Pallas kernels  29.4 us (21%)
  waiting for transfers between devices  20.2 us (14%)
  starting transfers between devices  19.5 us (14%)
    all_to_all x4, blocking collectives, exchange(): lax.all_to_all(block, axis, 0, 0, axis_index_groups=groups, tiled=True)  69.9 us
    pallas_call x9, Pallas kernels, call(): pl.pallas_call(kernel, out_shape=out_shape, in_specs=in_specs, out_specs=...  29.4 us
    all_to_all x3, waiting for transfers between devices, exchange(): lax.all_to_all(block, axis, 0, 0, axis_index_groups=groups, tiled=True)  14.5 us
    all_to_all x3, starting transfers between devices, exchange(): lax.all_to_all(block, axis, 0, 0, axis_index_groups=groups, tiled=True)  10.7 us
    ppermute x4, starting transfers between devices, swap_cores(): return lax.ppermute(block, 'fsdp', [(i, i ^ 1) for i in range(2 * Z)])  5.79 us
    ppermute x4, waiting for transfers between devices, swap_cores(): return lax.ppermute(block, 'fsdp', [(i, i ^ 1) for i in range(2 * Z)])  3.39 us
    ppermute x3, starting transfers between devices, per_device(): received.append(lax.ppermute(gram_part, 'tensor', pairs))  3.07 us
  transfers between devices with their start and end apart: 10, of which 9 were waited for; matrix products, arithmetic and copies ran while one was open for 0% of the time, Pallas kernels for 8%

commit v1 on v0

--- a/solution.py
+++ b/solution.py
@@ -204,6 +204,16 @@
     out_ref[...] = total
 
 
+def rows_kernel(left_ref, kept_ref, given_ref, square_ref):
+    turned = terms(left_ref[...].T, 3)
+    square_ref[...] = term_multiply(turned, turned, 1)
+    core = own_place()[1]
+    size = kept_ref.shape[0]
+    for target, half in ((kept_ref, core), (given_ref, 1 - core)):
+        start = (lax.axis_index("tensor") * 2 + half) * size
+        target[...] = square_ref[pl.ds(pl.multiple_of(start, size), size), :]
+
+
 def first_kernel(
     gram_ref, left_ref, momentum_ref, gradient_ref,
     once_ref, kept_ref, given_ref, work_ref, inverse_ref, square_ref, right_ref,
@@ -379,22 +389,7 @@
     return lax.ppermute(block, "fsdp", [(i, i ^ 1) for i in range(2 * Z)])
 
 
-def core_half(block, core):
-    half = block.shape[0] // 2
-    kept = lax.dynamic_slice_in_dim(block, core * half, half)
-    given = lax.dynamic_slice_in_dim(block, (1 - core) * half, half)
-    return kept + swap_cores(given)
-
-
-def gram_rows(factor, place):
-    width = RANK // TENSOR
-    own = lax.dynamic_slice_in_dim(factor, place * width, width, axis=1)
-    return multiply(own, factor, 0, 0)
-
-
 def per_device(momentum, gradient, right_state):
-    core = lax.axis_index("fsdp") % 2
-    place = lax.axis_index("tensor")
     rows, columns = momentum.shape
     held = [room(rows, columns), room(rows, columns, dtype=gradient.dtype)]
     (partial_left,) = call(
@@ -409,7 +404,9 @@
     (parts,) = call(sum_kernel, "left_sum", (parts,), (parts.shape,))
     left_raw = exchange(parts, "tensor").reshape(rows, RANK)
 
-    gram_part = core_half(gram_rows(left_raw, place), core)
+    share = (RANK // (2 * TENSOR), RANK)
+    kept, given = call(rows_kernel, "rows", (left_raw,), (share, share), [room(RANK, RANK)])
+    gram_part = kept + swap_cores(given)
     parts = exchange(copies(gram_part, Z), "fsdp", z_groups)
     (parts,) = call(
         sum_kernel, "gram_sum", (parts,), ((2 * TENSOR,) + parts.shape[1:],)

time: 141 us -> 140 us (level)
  blocking collectives: 69.9 us -> 83 us
  waiting for transfers between devices: 20.2 us -> 10.6 us
  starting transfers between devices: 19.5 us -> 15.7 us
    all_to_all x4 -> x5, blocking collectives: 69.9 us -> 83 us  [exchange(): lax.all_to_all(block, axis, 0, 0, axis_index_groups=groups, tiled=True)]
    all_to_all x3 -> x2, waiting for transfers between devices: 14.5 us -> 4.89 us  [exchange(): lax.all_to_all(block, axis, 0, 0, axis_index_groups=groups, tiled=True)]
    all_to_all x3 -> x2, starting transfers between devices: 10.7 us -> 7.11 us  [exchange(): lax.all_to_all(block, axis, 0, 0, axis_index_groups=groups, tiled=True)]
    pallas_call x9 -> x10, Pallas kernels: 29.4 us -> 29.3 us  [call(): pl.pallas_call(kernel, out_shape=out_shape, in_specs=in_specs, out_specs=...]
  transfers between devices with their start and end apart: 10 -> 9, of which waited for: 9 -> 8; matrix products, arithmetic and copies ran while one was open for 0% -> 0% of each run, Pallas kernels for 8% -> 8%
where the time goes in v1:
time: 140 us
  blocking collectives  83 us (59%)
  Pallas kernels  29.3 us (21%)
  starting transfers between devices  15.7 us (11%)
  waiting for transfers between devices  10.6 us (8%)
    all_to_all x5, blocking collectives, exchange(): lax.all_to_all(block, axis, 0, 0, axis_index_groups=groups, tiled=True)  83 us
    pallas_call x10, Pallas kernels, call(): pl.pallas_call(kernel, out_shape=out_shape, in_specs=in_specs, out_specs=...  29.3 us
    all_to_all x2, starting transfers between devices, exchange(): lax.all_to_all(block, axis, 0, 0, axis_index_groups=groups, tiled=True)  7.11 us
    ppermute x4, starting transfers between devices, swap_cores(): return lax.ppermute(block, 'fsdp', [(i, i ^ 1) for i in range(2 * Z)])  5.51 us
    all_to_all x2, waiting for transfers between devices, exchange(): lax.all_to_all(block, axis, 0, 0, axis_index_groups=groups, tiled=True)  4.89 us
    ppermute x4, waiting for transfers between devices, swap_cores(): return lax.ppermute(block, 'fsdp', [(i, i ^ 1) for i in range(2 * Z)])  3.4 us
    ppermute x3, starting transfers between devices, per_device(): received.append(lax.ppermute(gram_part, 'tensor', pairs))  3.04 us
  transfers between devices with their start and end apart: 9, of which 8 were waited for; matrix products, arithmetic and copies ran while one was open for 0% of the time, Pallas kernels for 8%

profile of v1, /device:TPU:1, one launch (start us, length us, event | category | flops | bytes accessed | tf_op | source)
XLA Modules:
  0.0 139.7 jit_solution(8865566790741055793)
XLA Ops:
  0.6 3.6 %left.1 = f32[512,256]{1,0:T(8,128)S(1)} custom-call(f32[512,896]{1,0:T(8,128)} %momentum_ref.5, bf16[512,896]{1,0:T(8,128)(2,1)} %gradient_ref.5, f32[896,256]{1,0:T(8,128)} %state_ref.1), custom_call_target="tpu_custom_call" | custom-call | flops 1000000000 | bytes 8388608 | tf_op jit(solution)/shard_map/left/pallas_call | solution.py:356
  4.2 17.9 %all_to_all.35.parts_ref = f32[16,32,256]{2,1,0:T(8,128)S(1)} all-to-all(f32[16,32,256]{2,1,0:T(8,128)S(1)} %bitcast.5), channel_id=1, replica_groups=mesh['fsdp'=16,'tensor'=16] {'tensor'}, dimensions={0} | all-to-all | bytes 1048576 | tf_op jit(solution)/shard_map/all_to_all | solution.py:381
  22.1 0.1 left_sum.1
  22.2 13.1 %all_to_all.36 = f32[16,32,256]{2,1,0:T(8,128)S(1)} all-to-all(f32[16,32,256]{2,1,0:T(8,128)S(1)} %left_sum.1), channel_id=1, replica_groups=mesh['fsdp'=16,'tensor'=16] {'tensor'}, dimensions={0} | all-to-all | bytes 1048576 | tf_op jit(solution)/shard_map/all_to_all | solution.py:381
  35.3 0.7 rows.1
  36.0 2.7 %collective-permute-start = (f32[8,256]{1,0:T(8,128)S(1)}, f32[8,256]{1,0:T(8,128)S(1)}, u32[]{:S(2)}, u32[]{:S(2)}) collective-permute-start(f32[8,256]{1,0:T(8,128)S(1)} %get-tuple-element.17), channel_id=1, source_target_pairs={{0,16},{16,0},{32,48},{48,32},{64,80},{80,64},{96,112},{112,96},{1... | collective-permute-start | bytes 24584 | tf_op jit(solution)/shard_map/ppermute | solution.py:389
  38.6 0.8 collective-permute-done
  39.5 15.2 %all_to_all.37.parts_ref = f32[8,8,256]{2,1,0:T(8,128)S(1)} all-to-all(f32[8,8,256]{2,1,0:T(8,128)S(1)} %broadcast_in_dim.6), channel_id=1, replica_groups={{0,32,64,96,128,160,192,224},{16,48,80,112,144,176,208,240},{1,33,65,97..., dimensions={0} | all-to-all | bytes 131072 | tf_op jit(solution)/shard_map/all_to_all | solution.py:381
  54.7 13.6 %all_to_all.38 = f32[32,8,256]{2,1,0:T(8,128)S(1)} all-to-all(f32[32,8,256]{2,1,0:T(8,128)S(1)} %gram_sum.1), channel_id=1, replica_groups={{0,16,1,17,2,18,3,19,4,20,5,21,6,22,7,23,8,24,9,25,10,26,11,27,12,28,13..., dimensions={0} | all-to-all | bytes 524288 | tf_op jit(solution)/shard_map/all_to_all | solution.py:381
  68.4 10.1 %first.1 = (f32[512,256]{1,0:T(8,128)S(1)}, f32[472,256]{1,0:T(8,128)S(1)}, f32[472,256]{1,0:T(8,128)S(1)}) custom-call(f32[256,256]{1,0:T(8,128)S(1)} %bitcast.9, f32[512,256]{1,0:T(8,128)S(1)} %bitcast.7, f32[512,896]{1,0:T(8,128)} %momentum_ref.5, bf16[512,896]{1,0:T(8,128)(2,1)} %gradient_ref.5), custom_call_target="tpu_custom_call" | custom-call | flops 1000000000 | bytes 8388608 | tf_op jit(solution)/shard_map/first/pallas_call | solution.py:356
  78.4 0.5 collective-permute-start.1
  78.9 1.6 %collective-permute-done.1 = f32[472,256]{1,0:T(8,128)S(1)} collective-permute-done((f32[472,256]{1,0:T(8,128)S(1)}, f32[472,256]{1,0:T(8,128)S(1)}, u32[]{:S(2)}, u32[]{:S(2)}) %collective-permute-start.1) | collective-permute-done | bytes 483360 | tf_op jit(solution)/shard_map/ppermute | solution.py:389
  80.6 0.1 add.7
  80.7 0.1 pad_maximum_fusion
  80.8 23.2 %all_to_all.39.parts_ref = f32[8,80,256]{2,1,0:T(8,128)S(1)} all-to-all(f32[8,80,256]{2,1,0:T(8,128)S(1)} %pad_maximum_fusion), channel_id=1, replica_groups={{0,32,64,96,128,160,192,224},{16,48,80,112,144,176,208,240},{1,33,65,97..., dimensions={0} | all-to-all | bytes 1310720 | tf_op jit(solution)/shard_map/all_to_all | solution.py:381
  103.9 0.8 right_sum.1
  104.8 3.5 %all-to-all-start.5 = ((f32[8,56,256]{2,1,0:T(8,128)}), f32[8,56,256]{2,1,0:T(8,128)S(1)}, u32[]{:S(2)}, u32[]{:S(2)}) async-start(f32[8,56,256]{2,1,0:T(8,128)} %get-tuple-element.20), calls=%async_computation.5 | async-start | bytes 917504 | tf_op jit(solution)/shard_map/all_to_all | solution.py:381
  108.2 0.5 collective-permute-start.2
  108.8 1.9 %collective-permute-start.3 = (f32[24,256]{1,0:T(8,128)S(1)}, f32[24,256]{1,0:T(8,128)S(1)}, u32[]{:S(2)}, u32[]{:S(2)}) collective-permute-start(f32[24,256]{1,0:T(8,128)S(1)} %get-tuple-element.21), channel_id=1, source_target_pairs={{0,2},{1,3},{2,0},{3,1},{4,6},{5,7},{6,4},{7,5},{8,10},{9,11},{10,... | collective-permute-start | bytes 73736 | tf_op jit(solution)/shard_map/ppermute | solution.py:439
  110.6 0.6 collective-permute-start.4
  111.3 0.9 collective-permute-done.2
  112.2 0.8 collective-permute-done.3
  113.1 0.6 collective-permute-done.4
  113.6 1.9 %collective-permute-start.5 = (f32[96,256]{1,0:T(8,128)S(1)}, f32[96,256]{1,0:T(8,128)S(1)}, u32[]{:S(2)}, u32[]{:S(2)}) collective-permute-start(f32[96,256]{1,0:T(8,128)S(1)} %constant_dynamic-update-slice_fusion.own_ref), channel_id=1, source_target_pairs={{0,16},{16,0},{32,48},{48,32},{64,80},{80,64},{96,112},{112,96},{1... | collective-permute-start | bytes 294920 | tf_op jit(solution)/shard_map/ppermute | solution.py:389
  115.5 0.9 collective-permute-done.5.other_ref
  116.4 6.9 %second.1.found_ref = f32[768,256]{1,0:T(8,128)S(1)} custom-call(f32[96,256]{1,0:T(8,128)S(1)} %constant_dynamic-update-slice_fusion.own_ref, f32[96,256]{1,0:T(8,128)S(1)} %collective-permute-done.5.other_ref, f32[512,256]{1,0:T(8,128)S(1)} %get-tuple-element.22.once_ref), custom_call_target="tpu_custom_call" | custom-call | flops 1000000000 | bytes 8388608 | tf_op jit(solution)/shard_map/second/pallas_call | solution.py:356
  123.4 1.4 all-to-all-done.5
  124.7 1.2 third.1
  125.9 0.5 collective-permute-start.6
  126.4 3.6 %all-to-all-start.6 = ((f32[32,1,256]{2,1,0:T(1,128)}), f32[32,1,256]{2,1,0:T(1,128)S(1)}, u32[]{:S(2)}, u32[]{:S(2)}) async-start(f32[32,1,256]{2,1,0:T(1,128)} %get-tuple-element.26), calls=%async_computation.6 | async-start | bytes 65536 | tf_op jit(solution)/shard_map/all_to_all | solution.py:381
  130.0 0.0 collective-permute-done.6.other_ref
  130.1 3.7 %fourth.1 = f32[512,896]{1,0:T(8,128)} custom-call(f32[512,896]{1,0:T(8,128)} %momentum_ref.5, bf16[512,896]{1,0:T(8,128)(2,1)} %gradient_ref.5, f32[768,256]{1,0:T(8,128)S(1)} %second.1.found_ref, f32[448,256]{1,0:T(8,128)S(1)} %get-tuple-element.25.own_ref, f32[448,256]{1,0:T(8,128)S(1)} %collective-permute-done.6.other_ref), custom_call_target="tpu_custom_call" | custom-call | flops 1000000000 | bytes 8388608 | tf_op jit(solution)/shard_map/fourth/pallas_call | solution.py:356
  133.8 3.5 %all-to-all-done.6.squares_ref = f32[32,1,256]{2,1,0:T(1,128)S(1)} async-done(((f32[32,1,256]{2,1,0:T(1,128)}), f32[32,1,256]{2,1,0:T(1,128)S(1)}, u32[]{:S(2)}, u32[]{:S(2)}) %all-to-all-start.6) | async-done | bytes 32800 | tf_op jit(solution)/shard_map/all_to_all | solution.py:381
  137.3 2.3 %fifth.1 = (f32[896,256]{1,0:T(8,128)}, f32[512,896]{1,0:T(8,128)}) custom-call(f32[32,1,256]{2,1,0:T(1,128)S(1)} %all-to-all-done.6.squares_ref, f32[768,256]{1,0:T(8,128)S(1)} %second.1.found_ref, f32[448,256]{1,0:T(8,128)S(1)} %get-tuple-element.25.own_ref, f32[448,256]{1,0:T(8,128)S(1)} %collective-permute-done.6.other_ref), custom_call_target="tpu_custom_call" | custom-call | flops 1000000000 | bytes 8388608 | tf_op jit(solution)/shard_map/fifth/pallas_call | solution.py:356
  (10 shorter events, 0.1 us)
Async XLA Ops:
  36.0 3.5 %collective-permute-start = (f32[8,256]{1,0:T(8,128)S(1)}, f32[8,256]{1,0:T(8,128)S(1)}, u32[]{:S(2)}, u32[]{:S(2)}) collective-permute-start(f32[8,256]{1,0:T(8,128)S(1)} %get-tuple-element.17), channel_id=1, source_target_pairs={{0,16},{16,0},{32,48},{48,32},{64,80},{80,64},{96,112},{112,96},{1... | collective-permute-start | bytes 24584 | tf_op jit(solution)/shard_map/ppermute | solution.py:389
  78.4 2.1 %collective-permute-start.1 = (f32[472,256]{1,0:T(8,128)S(1)}, f32[472,256]{1,0:T(8,128)S(1)}, u32[]{:S(2)}, u32[]{:S(2)}) collective-permute-start(f32[472,256]{1,0:T(8,128)S(1)} %get-tuple-element.19), channel_id=1, source_target_pairs={{0,16},{16,0},{32,48},{48,32},{64,80},{80,64},{96,112},{112,96},{1... | collective-permute-start | bytes 1449992 | tf_op jit(solution)/shard_map/ppermute | solution.py:389
  104.8 20.0 %all-to-all-start.5 = ((f32[8,56,256]{2,1,0:T(8,128)}), f32[8,56,256]{2,1,0:T(8,128)S(1)}, u32[]{:S(2)}, u32[]{:S(2)}) async-start(f32[8,56,256]{2,1,0:T(8,128)} %get-tuple-element.20), calls=%async_computation.5 | async-start | bytes 917504 | tf_op jit(solution)/shard_map/all_to_all | solution.py:381
  108.2 4.0 %collective-permute-start.2 = (f32[24,256]{1,0:T(8,128)S(1)}, f32[24,256]{1,0:T(8,128)S(1)}, u32[]{:S(2)}, u32[]{:S(2)}) collective-permute-start(f32[24,256]{1,0:T(8,128)S(1)} %get-tuple-element.21), channel_id=1, source_target_pairs={{0,1},{1,2},{2,3},{3,0},{4,5},{5,6},{6,7},{7,4},{8,9},{9,10},{10,1... | collective-permute-start | bytes 73736 | tf_op jit(solution)/shard_map/ppermute | solution.py:439
  108.8 4.3 %collective-permute-start.3 = (f32[24,256]{1,0:T(8,128)S(1)}, f32[24,256]{1,0:T(8,128)S(1)}, u32[]{:S(2)}, u32[]{:S(2)}) collective-permute-start(f32[24,256]{1,0:T(8,128)S(1)} %get-tuple-element.21), channel_id=1, source_target_pairs={{0,2},{1,3},{2,0},{3,1},{4,6},{5,7},{6,4},{7,5},{8,10},{9,11},{10,... | collective-permute-start | bytes 73736 | tf_op jit(solution)/shard_map/ppermute | solution.py:439
  110.6 3.0 %collective-permute-start.4 = (f32[24,256]{1,0:T(8,128)S(1)}, f32[24,256]{1,0:T(8,128)S(1)}, u32[]{:S(2)}, u32[]{:S(2)}) collective-permute-start(f32[24,256]{1,0:T(8,128)S(1)} %get-tuple-element.21), channel_id=1, source_target_pairs={{0,3},{1,0},{2,1},{3,2},{4,7},{5,4},{6,5},{7,6},{8,11},{9,8},{10,9... | collective-permute-start | bytes 73736 | tf_op jit(solution)/shard_map/ppermute | solution.py:439
  113.6 2.8 %collective-permute-start.5 = (f32[96,256]{1,0:T(8,128)S(1)}, f32[96,256]{1,0:T(8,128)S(1)}, u32[]{:S(2)}, u32[]{:S(2)}) collective-permute-start(f32[96,256]{1,0:T(8,128)S(1)} %constant_dynamic-update-slice_fusion.own_ref), channel_id=1, source_target_pairs={{0,16},{16,0},{32,48},{48,32},{64,80},{80,64},{96,112},{112,96},{1... | collective-permute-start | bytes 294920 | tf_op jit(solution)/shard_map/ppermute | solution.py:389
  125.9 4.1 %collective-permute-start.6 = (f32[448,256]{1,0:T(8,128)S(1)}, f32[448,256]{1,0:T(8,128)S(1)}, u32[]{:S(2)}, u32[]{:S(2)}) collective-permute-start(f32[448,256]{1,0:T(8,128)S(1)} %get-tuple-element.25.own_ref), channel_id=1, source_target_pairs={{0,16},{16,0},{32,48},{48,32},{64,80},{80,64},{96,112},{112,96},{1... | collective-permute-start | bytes 1376264 | tf_op jit(solution)/shard_map/ppermute | solution.py:389
  126.4 10.9 %all-to-all-start.6 = ((f32[32,1,256]{2,1,0:T(1,128)}), f32[32,1,256]{2,1,0:T(1,128)S(1)}, u32[]{:S(2)}, u32[]{:S(2)}) async-start(f32[32,1,256]{2,1,0:T(1,128)} %get-tuple-element.26), calls=%async_computation.6 | async-start | bytes 65536 | tf_op jit(solution)/shard_map/all_to_all | solution.py:381
